TPU v7x, 128 devices: a whole 4x4x4 slice. The times are simulated.
128 devices in a mesh: batch: 2 (over x_lo), tensor: 8 (over z, core), grid: 8 (over x_hi, y).
Axes of the slice: x: 4 (x_hi: 2, x_lo: 2; x = x_hi * 2 + x_lo), y: 4, z: 4, core: 2. Of those that a mesh axis runs over, the one named last changes fastest.
Arguments:
- gate_pre: bfloat16 [2048, 27648], P(('batch', 'grid'), 'tensor'), may hold values from -6 to 6
- up_pre: bfloat16 [2048, 27648], P(('batch', 'grid'), 'tensor'), may hold values from -6 to 6
- out_grad: bfloat16 [2048, 5120], P(('batch', 'grid'), 'tensor'), may hold values from -0.59765625 to 0.59765625
- basis_in: bfloat16 [27648, 14336], P('tensor', ('batch', 'grid')), may hold values from -0.0390625 to 0.0390625
- basis_out: bfloat16 [5120, 5120], P('tensor'), may hold values from -0.078125 to 0.078125
- lengths: int32 [8], replicated, may hold values from 1 to 512, 2048 in all
Outputs:
- eigenvalues: float32 [5120, 14336], P('tensor', ('batch', 'grid'))
Inputs may be any that keep to these rules, and one draw needn't show every extreme that they name: `lengths`: the 8 sequences are packed in order and fill all 2048 rows; the longest has exactly 512 tokens.
All inputs are finite; a program needn't handle non-finite values.
Results may differ from a plain program's by a relative error of at most 0.0039.
Values may be sent and summed in bfloat16 or wider, within the bound.
A program may use at most 128 MiB of HBM per device.

v0:
```python
import jax
import jax.numpy as jnp
from jax import lax
from jax.sharding import PartitionSpec as P

MAXLEN = 512


def shards(gate_pre, up_pre, out_grad, basis_in, basis_out, lengths):
    activations = (jax.nn.silu(gate_pre.astype(jnp.float32)) * up_pre.astype(jnp.float32)).astype(
        jnp.bfloat16
    )
    partial_in = jnp.dot(
        lax.all_gather(activations, ("batch", "grid"), axis=0, tiled=True),
        basis_in,
        preferred_element_type=jnp.float32,
    )
    rotated = lax.psum(partial_in, "tensor").astype(jnp.bfloat16)
    grad_share = lax.psum_scatter(
        lax.dot_general(
            basis_out, out_grad, (((0,), (1,)), ((), ())), preferred_element_type=jnp.float32
        ),
        "tensor",
        scatter_dimension=0,
        tiled=True,
    )
    grad_rotated = lax.all_gather(
        grad_share.astype(jnp.bfloat16), ("batch", "grid"), axis=1, tiled=True
    )
    seq_total = lengths.shape[0]
    offsets = jnp.cumsum(lengths) - lengths
    rotated_pad = jnp.concatenate([rotated, jnp.zeros((MAXLEN, rotated.shape[1]), jnp.bfloat16)], 0)
    grad_pad = jnp.concatenate(
        [grad_rotated, jnp.zeros((grad_rotated.shape[0], MAXLEN), jnp.bfloat16)], 1
    )
    zeros_block = jnp.zeros((grad_rotated.shape[0], rotated.shape[1]), jnp.float32)

    def window_product(begin_row, live_rows, span_rows):
        slab_in = lax.dynamic_slice_in_dim(rotated_pad, begin_row, span_rows, 0)
        row_keep = (jnp.arange(span_rows, dtype=jnp.int32) < live_rows)[:, None]
        slab_in = jnp.where(row_keep, slab_in, jnp.zeros_like(slab_in))
        slab_out = lax.dynamic_slice_in_dim(grad_pad, begin_row, span_rows, 1)
        return jnp.dot(slab_out, slab_in, preferred_element_type=jnp.float32)

    def add_sequence(sequence, totals):
        product = window_product(offsets[sequence], lengths[sequence], MAXLEN)
        return totals + product * product

    totals = lax.fori_loop(0, seq_total, add_sequence, zeros_block)
    return totals / seq_total


def solution(mesh):
    return jax.shard_map(
        shards,
        mesh=mesh,
        in_specs=(
            P(("batch", "grid"), "tensor"),
            P(("batch", "grid"), "tensor"),
            P(("batch", "grid"), "tensor"),
            P("tensor", ("batch", "grid")),
            P("tensor", None),
            P(),
        ),
        out_specs=P("tensor", ("batch", "grid")),
        check_vma=False,
    )
```

profile of v0, /device:TPU:1, one launch (start us, length us, event | category | flops | bytes accessed | tf_op | source)
XLA Modules:
  0.0 455.9 jit_solution(5998761373173624271)
XLA Ops:
  6.5 0.9 copy-done
  7.5 6.3 %fusion.12 = f32[5120,128]{1,0:T(8,128)} fusion(bf16[640,5120]{1,0:T(8,128)(2,1)} %param.12, bf16[128,640]{1,0:T(8,128)(2,1)S(1)} %copy-done), kind=kOutput, calls=%fused_computation.18 | convolution fusion | flops 838860800 | bytes 9338880 | tf_op jit(solution)/shard_map/dot_general | solution.py:20
  13.8 0.0 all-gather.3.cloned.1.call-start
  13.8 35.0 %reduce-scatter.2.cloned.1.call-done = f32[640,128]{1,0:T(8,128)} async-done(((f32[5120,128]{1,0:T(8,128)}), f32[640,128]{1,0:T(8,128)}) %reduce-scatter.2.cloned.1.call-update) | async-done | bytes 327696 | tf_op jit(solution)/shard_map/reduce_scatter | solution.py:19
  48.8 1.7 convert_element_type.15
  50.5 0.0 all-gather.5.cloned.1.call-start
  50.6 1.4 fusion.11
  52.1 0.2 reduce-window.9
  52.3 67.5 %all-gather.3.cloned.1.call-done = bf16[640,2048]{1,0:T(8,128)(2,1)} async-done(((bf16[640,128]{1,0:T(8,128)(2,1)}), bf16[640,2048]{1,0:T(8,128)(2,1)}) %all-gather.3.cloned.1.call-update) | async-done | bytes 2621456 | tf_op jit(solution)/shard_map/all_gather | solution.py:27
  119.7 3.7 concatenate.6
  123.4 164.7 %all-gather.5.cloned.1.call-done = bf16[2048,3456]{1,0:T(8,128)(2,1)} async-done(((bf16[128,3456]{1,0:T(8,128)(2,1)}), bf16[2048,3456]{1,0:T(8,128)(2,1)}) %all-gather.5.cloned.1.call-update) | async-done | bytes 14155792 | tf_op jit(solution)/shard_map/all_gather | solution.py:14
  288.1 20.7 %fusion.13 = f32[2048,896]{1,0:T(8,128)} fusion(bf16[2048,3456]{1,0:T(8,128)(2,1)} %all-gather.5.cloned.1.call-done, bf16[3456,896]{1,0:T(8,128)(2,1)} %param.11), kind=kOutput, calls=%fused_computation.19 | convolution fusion | flops 12683575296 | bytes 27688960 | tf_op jit(solution)/shard_map/dot_general | solution.py:13
  308.8 80.8 %all-reduce.3 = bf16[2048,896]{1,0:T(8,128)(2,1)} all-reduce(f32[2048,896]{1,0:T(8,128)} %fusion.13), channel_id=1, replica_groups=mesh['batch'=2,'tensor'=8,'grid'=8] {'tensor'}, use_global_device_ids=true, to_apply=%region_1.2 | all-reduce | flops 1835008 | bytes 11010048 | tf_op jit(solution)/shard_map/psum | solution.py:18
  389.7 4.5 concatenate.7
  394.1 53.7 %while.14 = (s32[]{:T(128)}, f32[640,896]{1,0:T(8,128)S(1)}, s32[8]{0:T(128)S(1)}, bf16[640,2560]{1,0:T(8,128)(2,1)}, s32[8]{0:T(128)S(1)}, /*index=5*/bf16[2560,896]{1,0:T(8,128)(2,1)}, s32[]{:T(128)}, s32[]{:T(128)}, s32[]{:T(128)}) while((s32[]{:T(128)}, f32[640,896]{1,0:T(8,128)S(1)}, s32[8]{0:T(128)S(1)}, ...), condition=%wide.region_4.5_spmd.clone, body=%wide.region_3.4_spmd.clone.sunk | while | flops 589382144 | bytes 6163108 | solution.py:49
  394.1 0.6 dynamic_slice.44
  396.6 0.6 dynamic_slice.45
  397.2 0.6 iota_compare_fusion.2
  397.9 2.9 select_add_fusion.2
  400.8 0.6 dynamic_slice.44
  403.4 0.6 dynamic_slice.45
  404.0 0.6 iota_compare_fusion.2
  404.6 2.9 select_add_fusion.2
  407.6 0.6 dynamic_slice.44
  410.1 0.6 dynamic_slice.45
  410.7 0.6 iota_compare_fusion.2
  411.3 2.9 select_add_fusion.2
  414.3 0.6 dynamic_slice.44
  416.8 0.6 dynamic_slice.45
  417.4 0.6 iota_compare_fusion.2
  418.1 2.9 select_add_fusion.2
  421.0 0.6 dynamic_slice.44
  423.5 0.6 dynamic_slice.45
  424.1 0.6 iota_compare_fusion.2
  424.8 2.9 select_add_fusion.2
  427.7 0.6 dynamic_slice.44
  430.2 0.6 dynamic_slice.45
  430.8 0.6 iota_compare_fusion.2
  431.5 2.9 select_add_fusion.2
  434.4 0.6 dynamic_slice.44
  437.0 0.6 dynamic_slice.45
  437.6 0.6 iota_compare_fusion.2
  438.2 2.9 select_add_fusion.2
  441.2 0.6 dynamic_slice.44
  443.7 0.6 dynamic_slice.45
  444.3 0.6 iota_compare_fusion.2
  444.9 2.9 select_add_fusion.2
  447.9 1.5 broadcast_multiply_fusion
  (13 shorter events, 0.1 us)
Async XLA Ops:
  6.5 0.9 copy-start
  6.5 42.3 %reduce-scatter.2.cloned.1.call-start = ((), (), s32[]{:S(2)}) async-start(), calls=%async_computation.1 | async-start | bytes 2949120 | tf_op jit(solution)/shard_map/reduce_scatter | solution.py:19
  13.7 36.8 %copy-start.1 = (bf16[128,3456]{1,0:T(8,128)(2,1)S(1)}, bf16[128,3456]{1,0:T(8,128)(2,1)}, u32[]{:S(2)}) copy-start(bf16[128,3456]{1,0:T(8,128)(2,1)} %param.9) | copy-start | bytes 2654212
  13.7 36.8 %copy-start.2 = (bf16[128,3456]{1,0:T(8,128)(2,1)S(1)}, bf16[128,3456]{1,0:T(8,128)(2,1)}, u32[]{:S(2)}) copy-start(bf16[128,3456]{1,0:T(8,128)(2,1)} %param.8) | copy-start | bytes 2654212
  13.8 38.3 %copy-start.3 = (s32[8]{0:T(128)S(1)}, s32[8]{0:T(128)}, u32[]{:S(2)}) copy-start(s32[8]{0:T(128)} %param.13) | copy-start | bytes 100
  13.8 105.9 %all-gather.3.cloned.1.call-start = ((), (), s32[]{:S(2)}) async-start(), calls=%async_computation.2 | async-start | bytes 2785280 | tf_op jit(solution)/shard_map/all_gather | solution.py:27
  50.5 237.6 %all-gather.5.cloned.1.call-start = ((), (), s32[]{:S(2)}) async-start(), calls=%async_computation.3 | async-start | bytes 15040512 | tf_op jit(solution)/shard_map/all_gather | solution.py:14
Sparse Core Ops, SparseCore 0:
  13.9 34.8 reduce-scatter.1
  50.6 69.0 all-gather.2
  121.4 166.6 all-gather.4
where the time goes:
time: 457 us; the launch traced here: 456 us
  waiting for transfers between devices  267 us (58%)
  blocking collectives  80.8 us (18%)
  matrix products  50.4 us (11%)
  local copies, waits for them, and re-layouts  18.5 us (4%)
  loops' own time  15.8 us (3%)
  between operations  13.2 us (3%)
  other arithmetic  10 us (2%)
    all_gather x1, waiting for transfers between devices, shards(): lax.all_gather(activations, ('batch', 'grid'), axis=0, tiled=True)  165 us
    psum x1, blocking collectives, shards(): rotated = lax.psum(partial_in, 'tensor').astype(jnp.bfloat16)  80.8 us
    all_gather x1, waiting for transfers between devices, shards(): lax.all_gather(grad_share.astype(jnp.bfloat16), ('batch', 'grid'), axis=1...  67.5 us
    reduce_scatter x1, waiting for transfers between devices, shards(): lax.psum_scatter(lax.dot_general(basis_out, out_grad, (((0,), (1,)), ((),...  35 us
    dot_general x8, matrix products, window_product(): return jnp.dot(slab_out, slab_in, preferred_element_type=jnp.float32)  23.3 us
    dot_general x1, matrix products, shards(): jnp.dot(lax.all_gather(activations, ('batch', 'grid'), axis=0, tiled=True...  20.7 us
    another operation x1, loops' own time, shards(): totals = lax.fori_loop(0, seq_total, add_sequence, zeros_block)  15.8 us
    dynamic_slice x16, local copies, waits for them, and re-layouts, add_sequence(): product = window_product(offsets[sequence], lengths[sequence], MAXLEN)  9.39 us
  transfers between devices with their start and end apart: 3, of which 3 were waited for; matrix products, arithmetic and copies ran while one was open for 1% of the time, Pallas kernels for 0%

commit v1 on v0

v1 whole, which is shorter than its diff:
```python
import functools

import jax
import jax.numpy as jnp
from jax import lax
from jax.experimental import pallas as pl
from jax.experimental.pallas import tpu as pltpu
from jax.sharding import PartitionSpec as P

MESH = pl.DeviceIdType.MESH
BF = jnp.bfloat16
F32 = jnp.float32

TOK = 128
HALF = 64
QUART = 32
HID = 3456
COLS = 896
FEAT = 640
D = 5120
NT = 8
STEPS = 4
OWN = 8
PER = 6


def gather_kernel(
    gate_hbm, up_hbm, grad_hbm, bin_hbm, bout_hbm, r_hbm, gt_hbm,
    gate_v, up_v, grad_v, bin_v, bout_v,
    abuf, psend, precv, rbuf, gsend, grecv, gx, gy,
    load_sem, xy_send, xy_recv, rs_send, rs_recv, ag_send, ag_recv,
    gr_send, gr_recv, gg_send, gg_recv, out_sem,
):
    xl = lax.axis_index("batch")
    me = lax.axis_index("tensor")
    gi = lax.axis_index("grid")
    x = lax.div(gi, 4) * 2 + xl
    y = lax.rem(gi, 4)

    def at(dx, dy):
        xx = lax.rem(x + (dx + 4), 4)
        yy = lax.rem(y + (dy + 4), 4)
        return (lax.rem(xx, 2), me, lax.div(xx, 2) * 4 + yy)

    def block_of(dx, dy):
        b, _, g = at(dx, dy)
        return b * 8 + g

    def peer(k):
        return (xl, lax.rem(me + k, NT), gi)

    xp, xm, yp, ym = at(1, 0), at(-1, 0), at(0, 1), at(0, -1)

    loads = [
        pltpu.make_async_copy(s, d, load_sem.at[i])
        for i, (s, d) in enumerate(
            [(gate_hbm, gate_v), (up_hbm, up_v), (grad_hbm, grad_v), (bout_hbm, bout_v), (bin_hbm, bin_v)]
        )
    ]
    for c in loads:
        c.start()

    barrier = pltpu.get_barrier_semaphore()
    for dev in [xp, xm, yp, ym] + [peer(k) for k in range(1, NT)]:
        pl.semaphore_signal(barrier, inc=1, device_id=dev, device_id_type=MESH)
    pl.semaphore_wait(barrier, 4 + NT - 1)

    def remote(src, dst, ss, rs, dev):
        return pltpu.make_async_remote_copy(
            src_ref=src, dst_ref=dst, send_sem=ss, recv_sem=rs, device_id=dev, device_id_type=MESH
        )

    def piece(i, off=0, n=HALF):
        return abuf.at[pl.ds(pl.multiple_of(i * HALF + off, 16), n)]

    def xy(step, k):
        first = isinstance(step, int) and step < 0
        fwd = k % 4 >= 2
        minus = k % 2
        is_y = k >= 4
        if first:
            base = 4 if is_y else 0
            own, near, far = base, base + 1 + minus, base + 3
            dev = ((yp, ym) if is_y else (xp, xm))[minus]
        else:
            b = OWN + PER * step
            own = (4 if is_y else 0) + step
            near = b + (2 if is_y else 0) + minus
            far = b + 4 + (1 if is_y else 0)
            dev = ((xp, xm) if is_y else (yp, ym))[minus]
        if fwd:
            src, dst = piece(near, QUART * minus, QUART), piece(far, QUART * minus, QUART)
        else:
            src, dst = piece(own), piece(near)
        sem = k if first else 8 + 8 * step + k
        return remote(src, dst, xy_send.at[sem], xy_recv.at[sem], dev)

    def rs_copy(gran, row, m, k):
        there = lax.rem(me + k, NT)
        return remote(
            psend.at[pl.ds(pl.multiple_of(row + there * m, 16), m)],
            precv.at[k - 1, pl.ds(pl.multiple_of(lax.div(row, NT), 16), m)],
            rs_send.at[gran, k - 1], rs_recv.at[gran, k - 1], peer(k),
        )

    def ag_copy(gran, row, m, k):
        here = rbuf.at[pl.ds(pl.multiple_of(row + me * m, 16), m)]
        return remote(here, here, ag_send.at[gran, k - 1], ag_recv.at[gran, k - 1], peer(k))

    def ag_wait(gran, row, m, k):
        there = rbuf.at[pl.ds(pl.multiple_of(row + lax.rem(me + NT - k, NT) * m, 16), m)]
        remote(there, there, ag_send.at[gran, k - 1], ag_recv.at[gran, k - 1], peer(k)).wait_recv()

    def multiply(gran, row, n):
        rows = pl.ds(pl.multiple_of(row, 64), n)
        psend[rows, :] = jnp.dot(abuf[rows, :], bin_v[...], preferred_element_type=F32).astype(BF)
        for k in (4, 3, 5, 2, 6, 1, 7):
            rs_copy(gran, row, n // NT, k).start()

    def combine(gran, row, n):
        m = n // NT
        mine = pl.ds(pl.multiple_of(row + me * m, 16), m)
        total = psend[mine, :].astype(F32)
        for k in range(1, NT):
            rs_copy(gran, row, m, k).wait_recv()
            total = total + precv[k - 1, pl.ds(pl.multiple_of(lax.div(row, NT), 16), m), :].astype(F32)
        rbuf[mine, :] = total.astype(BF)
        for k in (4, 3, 5, 2, 6, 1, 7):
            ag_copy(gran, row, m, k).start()

    def store(i, block, half):
        return pltpu.make_async_copy(
            rbuf.at[pl.ds(pl.multiple_of(i * HALF, 64), HALF)],
            r_hbm.at[pl.ds(pl.multiple_of(block * TOK + half * HALF, 64), HALF)],
            out_sem.at[i],
        )

    def finish(gran, row, n):
        for k in range(1, NT):
            ag_wait(gran, row, n // NT, k)

    GH = FEAT // 2
    GQ = FEAT // 4

    def gg(phase, k):
        fwd = k % 4 >= 2
        minus = k % 2
        is_y = k >= 4
        buf = gy if is_y else gx
        if phase == 0:
            dev = ((yp, ym) if is_y else (xp, xm))[minus]
            if fwd:
                rows = pl.ds(GQ * minus, GQ)
                src, dst = buf.at[0, 1 + minus, rows], buf.at[0, 3, rows]
            else:
                src, dst = buf.at[0, 0], buf.at[0, 1 + minus]
        else:
            dev = ((xp, xm) if is_y else (yp, ym))[minus]
            if fwd:
                part = pl.ds(2 * minus, 2)
                src, dst = buf.at[1 + minus, part], buf.at[3, part]
            else:
                src, dst = buf.at[0], buf.at[1 + minus]
        sem = 8 * phase + k
        return remote(src, dst, gg_send.at[sem], gg_recv.at[sem], dev)

    def gr_copy(k):
        return remote(
            gsend.at[lax.rem(me + k, NT)], grecv.at[k - 1], gr_send.at[k - 1], gr_recv.at[k - 1], peer(k)
        )

    loads[0].wait()
    loads[1].wait()
    for half, i in ((0, 0), (1, 4)):
        g = gate_v[pl.ds(half * HALF, HALF), :].astype(F32)
        u = up_v[pl.ds(half * HALF, HALF), :].astype(F32)
        abuf[pl.ds(i * HALF, HALF), :] = (g / (1.0 + jnp.exp(-g)) * u).astype(BF)
        for k in (0, 1):
            xy(-1, 4 * half + k).start()

    loads[2].wait()
    loads[3].wait()

    def rotate(c, carry):
        cols = pl.ds(pl.multiple_of(c * FEAT, 128), FEAT)
        gsend[c] = jnp.dot(grad_v[...], bout_v[:, cols], preferred_element_type=F32).astype(BF)
        return carry

    lax.fori_loop(0, NT, rotate, 0)
    for k in (4, 3, 5, 2, 6, 1, 7):
        gr_copy(k).start()
    loads[4].wait()

    for k in (0, 1, 4, 5):
        xy(-1, k).wait_recv()
        xy(-1, k + 2).start()
    for k in (0, 1, 4, 5):
        xy(0, k).start()

    share = gsend[me].astype(F32)
    for k in range(1, NT):
        gr_copy(k).wait_recv()
        share = share + grecv[k - 1].astype(F32)
    share = share.T.astype(BF)
    gx[0, 0] = share[:GH]
    gy[0, 0] = share[GH:]
    for k in (0, 1, 4, 5):
        gg(0, k).start()

    for k in (2, 3, 6, 7):
        xy(-1, k).wait_recv()
    for k in (0, 1, 4, 5):
        xy(1, k).start()
    multiply(0, 0, 256)
    multiply(1, 256, 256)

    for k in (0, 1, 4, 5):
        gg(0, k).wait_recv()
        gg(0, k + 2).start()

    def step(j, carry):
        row = OWN * HALF + j * (PER * HALF)
        gran = 2 + 2 * j
        prev = jnp.where(j == 0, 0, row - PER * HALF)
        for k in (0, 1, 4, 5):
            xy(j, k).wait_recv()
            xy(j, k + 2).start()

        @pl.when(j < 2)
        def _():
            for k in (0, 1, 4, 5):
                xy(j + 2, k).start()

        @pl.when(j == 0)
        def _():
            for k in (2, 3, 6, 7):
                gg(0, k).wait_recv()
            for k in (0, 1, 4, 5):
                gg(1, k).start()

        @pl.when(j == 1)
        def _():
            for k in (0, 1, 4, 5):
                gg(1, k).wait_recv()
                gg(1, k + 2).start()

        multiply(gran, row, 256)

        @pl.when(j == 0)
        def _():
            combine(0, 0, 256)
            combine(1, 256, 256)

        @pl.when(j > 0)
        def _():
            combine(gran - 2, row - 384, 256)
            combine(gran - 1, row - 128, 128)

        for k in (2, 3, 6, 7):
            xy(j, k).wait_recv()
        multiply(gran + 1, row + 256, 128)
        return carry

    lax.fori_loop(0, STEPS, step, 0)
    last = OWN * HALF + (STEPS - 1) * PER * HALF
    combine(8, last, 256)
    combine(9, last + 256, 128)

    OFF = (0, -1, 1, 2)
    outs = []

    def put(c):
        c.start()
        outs.append(c)

    for k in (2, 3, 6, 7):
        gg(1, k).wait_recv()
    for a in range(4):
        for b in range(4):
            for buf, half, dx, dy in ((gx, 0, OFF[b], OFF[a]), (gy, 1, OFF[a], OFF[b])):
                put(
                    pltpu.make_async_copy(
                        buf.at[a, b],
                        gt_hbm.at[block_of(dx, dy), pl.ds(half * GH, GH)],
                        out_sem.at[32 + half * 16 + 4 * a + b],
                    )
                )
    for gran in range(2):
        finish(gran, 256 * gran, 256)
    for i in range(4):
        put(store(i, block_of(OFF[i], 0), 0))
        put(store(4 + i, block_of(0, OFF[i]), 1))
    for j in range(STEPS):
        row = OWN * HALF + j * PER * HALF
        b = OWN + PER * j
        finish(2 + 2 * j, row, 256)
        put(store(b, block_of(OFF[j], -1), 0))
        put(store(b + 1, block_of(OFF[j], 1), 0))
        put(store(b + 2, block_of(-1, OFF[j]), 1))
        put(store(b + 3, block_of(1, OFF[j]), 1))
        finish(3 + 2 * j, row + 256, 128)
        put(store(b + 4, block_of(OFF[j], 2), 0))
        put(store(b + 5, block_of(2, OFF[j]), 1))

    for k in range(8):
        xy(-1, k).wait_send()
        gg(0, k).wait_send()
        gg(1, k).wait_send()
    for j in range(STEPS):
        for k in range(8):
            xy(j, k).wait_send()
    for k in range(1, NT):
        gr_copy(k).wait_send()
        for gran in range(10):
            if gran < 2:
                row, n = 256 * gran, 256
            else:
                row, n = 512 + 384 * ((gran - 2) // 2) + 256 * (gran % 2), 128 if gran % 2 else 256
            rs_copy(gran, row, n // NT, k).wait_send()
            ag_copy(gran, row, n // NT, k).wait_send()
    for c in outs:
        c.wait()


def gather_call(gate, up, grad, basis_in, basis_out):
    vm = pltpu.VMEM
    dma = pltpu.SemaphoreType.DMA
    hbm = pl.BlockSpec(memory_space=pl.ANY)
    return pl.pallas_call(
        gather_kernel,
        out_shape=(
            jax.ShapeDtypeStruct((2048, COLS), BF),
            jax.ShapeDtypeStruct((16, FEAT, TOK), BF),
        ),
        in_specs=[hbm] * 5,
        out_specs=(hbm, hbm),
        scratch_shapes=[
            vm((TOK, HID), BF), vm((TOK, HID), BF), vm((TOK, FEAT), BF), vm((HID, COLS), BF), vm((FEAT, D), BF),
            vm((2048, HID), BF), vm((2048, COLS), BF), vm((NT - 1, 256, COLS), BF), vm((2048, COLS), BF),
            vm((NT, TOK, FEAT), BF), vm((NT - 1, TOK, FEAT), BF),
            vm((4, 4, FEAT // 2, TOK), BF), vm((4, 4, FEAT // 2, TOK), BF),
            dma((5,)), dma((40,)), dma((40,)), dma((10, 7)), dma((10, 7)), dma((10, 7)), dma((10, 7)),
            dma((7,)), dma((7,)), dma((16,)), dma((16,)), dma((64,)),
        ],
        compiler_params=pltpu.CompilerParams(
            collective_id=0, has_side_effects=True, vmem_limit_bytes=58 * 2**20
        ),
        name="rotate_gather",
    )(gate, up, grad, basis_in, basis_out)


KB = 256


def fit_kernel(lengths, r_ref, gt_ref, out_ref):
    out_ref[...] = jnp.zeros_like(out_ref)

    def add(s, begin):
        end = begin + lengths[s]
        first = lax.div(begin, KB)
        blocks = lax.div(end + KB - 1, KB) - first

        for n in (1, 2, 3):

            @pl.when(blocks == n)
            def _():
                row = pl.multiple_of(first * KB, KB)
                r = r_ref[pl.ds(row, n * KB), :]
                token = row + lax.broadcasted_iota(jnp.int32, r.shape, 0)
                r = jnp.where((token >= begin) & (token < end), r, jnp.zeros_like(r))
                g = jnp.concatenate([gt_ref[2 * first + i] for i in range(2 * n)], axis=1)
                p = jnp.dot(g, r, preferred_element_type=F32)
                out_ref[...] += p * p

        return end

    lax.fori_loop(0, 8, add, 0)
    out_ref[...] = out_ref[...] * 0.125


def fit_call(lengths, r, gt):
    whole = pl.BlockSpec(memory_space=pltpu.VMEM)
    return pl.pallas_call(
        fit_kernel,
        out_shape=jax.ShapeDtypeStruct((FEAT, COLS), F32),
        in_specs=[pl.BlockSpec(memory_space=pltpu.SMEM), whole, whole],
        out_specs=whole,
        compiler_params=pltpu.CompilerParams(vmem_limit_bytes=58 * 2**20),
        name="sequence_products",
    )(lengths, r, gt)


def shards(gate_pre, up_pre, out_grad, basis_in, basis_out, lengths):
    r, gt = gather_call(gate_pre, up_pre, out_grad, basis_in, basis_out)
    return fit_call(lengths, r, gt)


def solution(mesh):
    return jax.shard_map(
        shards,
        mesh=mesh,
        in_specs=(
            P(("batch", "grid"), "tensor"),
            P(("batch", "grid"), "tensor"),
            P(("batch", "grid"), "tensor"),
            P("tensor", ("batch", "grid")),
            P("tensor", None),
            P(),
        ),
        out_specs=P("tensor", ("batch", "grid")),
        check_vma=False,
    )
```

time: 457 us -> 140 us (0.31)
  waiting for transfers between devices: 267 us -> 0 us
  Pallas kernels: 0 us -> 140 us
  blocking collectives: 80.8 us -> 0 us
  matrix products: 50.4 us -> 0 us
  local copies, waits for them, and re-layouts: 18.5 us -> 0 us
  loops' own time: 15.8 us -> 0 us
  between operations: 13.2 us -> 0.01 us
  other arithmetic: 10 us -> 0 us
    all_gather x2 -> x0, waiting for transfers between devices: 232 us -> none  [the longest x1 165 us: shards(): lax.all_gather(activations, ('batch', 'grid'), axis=0, tiled=True)]
    pallas_call x0 -> x2, Pallas kernels: none -> 140 us  [the longest x1 129 us: gather_call(): pl.pallas_call(gather_kernel, out_shape=(jax.ShapeDtypeStruct((2048, COLS...]
    psum x1 -> x0, blocking collectives: 80.8 us -> none  [shards(): rotated = lax.psum(partial_in, 'tensor').astype(jnp.bfloat16)]
    dot_general x10 -> x0, matrix products: 50.4 us -> none  [the longest x8 23.3 us: window_product(): return jnp.dot(slab_out, slab_in, preferred_element_type=jnp.float32)]
    reduce_scatter x1 -> x0, waiting for transfers between devices: 35 us -> none  [shards(): lax.psum_scatter(lax.dot_general(basis_out, out_grad, (((0,), (1,)), ((),...]
    another operation x1 -> x0, loops' own time: 15.8 us -> none  [shards(): totals = lax.fori_loop(0, seq_total, add_sequence, zeros_block)]
    dynamic_slice x16 -> x0, local copies, waits for them, and re-layouts: 9.39 us -> none  [add_sequence(): product = window_product(offsets[sequence], lengths[sequence], MAXLEN)]
    concatenate x2 -> x0, local copies, waits for them, and re-layouts: 8.14 us -> none  [the longest x1 4.46 us: shards(): jnp.concatenate([rotated, jnp.zeros((MAXLEN, rotated.shape[1]), jnp.bfloa...]
  transfers between devices with their start and end apart: 3 -> 0, of which waited for: 3 -> 0; matrix products, arithmetic and copies ran while one was open for 1% -> 0% of each run, Pallas kernels for 0% -> 0%
where the time goes in v1:
time: 140 us
  Pallas kernels  140 us (100%)
    pallas_call x1, Pallas kernels, gather_call(): pl.pallas_call(gather_kernel, out_shape=(jax.ShapeDtypeStruct((2048, COLS...  129 us
    pallas_call x1, Pallas kernels, fit_call(): pl.pallas_call(fit_kernel, out_shape=jax.ShapeDtypeStruct((FEAT, COLS), F...  10.9 us

profile of v1, /device:TPU:1, one launch (start us, length us, event | category | flops | bytes accessed | tf_op | source)
XLA Modules:
  0.0 140.3 jit_solution(13819442008681713830)
XLA Ops:
  0.0 129.4 %rotate_gather.1 = (bf16[2048,896]{1,0:T(8,128)(2,1)}, bf16[16,640,128]{2,1,0:T(8,128)(2,1)}) custom-call(bf16[128,3456]{1,0:T(8,128)(2,1)} %gate_hbm.1, bf16[128,3456]{1,0:T(8,128)(2,1)} %up_hbm.1, bf16[128,640]{1,0:T(8,128)(2,1)} %grad_hbm.1, bf16[3456,896]{1,0:T(8,128)(2,1)} %bin_hbm.1, bf16[640,5120]{1,0:T(8,128)(2,1)} %bout_hbm.1), custom_call_target="tpu_custom_call" | custom-call | tf_op jit(solution)/shard_map/rotate_gather/pallas_call | solution.py:329
  129.4 10.9 %sequence_products.1 = f32[640,896]{1,0:T(8,128)} custom-call(s32[8]{0:T(128)} %lengths.1, bf16[2048,896]{1,0:T(8,128)(2,1)} %get-tuple-element.7.r_ref, bf16[16,640,128]{2,1,0:T(8,128)(2,1)} %get-tuple-element.8.gt_ref), custom_call_target="tpu_custom_call" | custom-call | tf_op jit(solution)/shard_map/sequence_products/pallas_call | solution.py:383

commit v2 on v1

v2 whole, which is shorter than its diff:
```python
import functools

import jax
import jax.numpy as jnp
from jax import lax
from jax.experimental import pallas as pl
from jax.experimental.pallas import tpu as pltpu
from jax.sharding import PartitionSpec as P

MESH = pl.DeviceIdType.MESH
BF = jnp.bfloat16
F32 = jnp.float32

TOK = 128
HALF = 64
QUART = 32
HID = 3456
COLS = 896
FEAT = 640
D = 5120
NT = 8
STEPS = 4
OWN = 8
PER = 6


def gather_kernel(
    gate_hbm, up_hbm, grad_hbm, bin_hbm, bout_hbm, r_hbm, gt_hbm,
    gate_v, up_v, grad_v, bin_v, bout_v,
    abuf, pbuf, crecv, zsend, zrecv, rbuf, gpart, gcrecv, gzsend, gzrecv, gx, gy,
    load_sem, xy_send, xy_recv, ce_send, ce_recv, rs_send, rs_recv, ag_send, ag_recv, cf_send, cf_recv,
    gr_send, gr_recv, gg_send, gg_recv, out_sem,
):
    xl = lax.axis_index("batch")
    me = lax.axis_index("tensor")
    gi = lax.axis_index("grid")
    x = lax.div(gi, 4) * 2 + xl
    y = lax.rem(gi, 4)
    z = lax.div(me, 2)
    core = lax.rem(me, 2)

    def at(dx, dy):
        xx = lax.rem(x + (dx + 4), 4)
        yy = lax.rem(y + (dy + 4), 4)
        return (lax.rem(xx, 2), me, lax.div(xx, 2) * 4 + yy)

    def block_of(dx, dy):
        b, _, g = at(dx, dy)
        return b * 8 + g

    def zpeer(k):
        return (xl, lax.rem(z + k, 4) * 2 + core, gi)

    partner = (xl, z * 2 + 1 - core, gi)
    xp, xm, yp, ym = at(1, 0), at(-1, 0), at(0, 1), at(0, -1)

    loads = [
        pltpu.make_async_copy(s, d, load_sem.at[i])
        for i, (s, d) in enumerate(
            [(gate_hbm, gate_v), (up_hbm, up_v), (grad_hbm, grad_v), (bout_hbm, bout_v), (bin_hbm, bin_v)]
        )
    ]
    for c in loads:
        c.start()

    barrier = pltpu.get_barrier_semaphore()
    for dev in [xp, xm, yp, ym, partner, zpeer(1), zpeer(2), zpeer(3)]:
        pl.semaphore_signal(barrier, inc=1, device_id=dev, device_id_type=MESH)
    pl.semaphore_wait(barrier, 8)

    def remote(src, dst, ss, rs, dev):
        return pltpu.make_async_remote_copy(
            src_ref=src, dst_ref=dst, send_sem=ss, recv_sem=rs, device_id=dev, device_id_type=MESH
        )

    def rows_at(i, n):
        return pl.ds(pl.multiple_of(i, 16), n)

    def piece(i, off=0, n=HALF):
        return abuf.at[rows_at(i * HALF + off, n)]

    def xy(step, k):
        first = isinstance(step, int) and step < 0
        fwd = k % 4 >= 2
        minus = k % 2
        is_y = k >= 4
        if first:
            base = 4 if is_y else 0
            own, near, far = base, base + 1 + minus, base + 3
            dev = ((yp, ym) if is_y else (xp, xm))[minus]
        else:
            b = OWN + PER * step
            own = (4 if is_y else 0) + step
            near = b + (2 if is_y else 0) + minus
            far = b + 4 + (1 if is_y else 0)
            dev = ((xp, xm) if is_y else (yp, ym))[minus]
        if fwd:
            src, dst = piece(near, QUART * minus, QUART), piece(far, QUART * minus, QUART)
        else:
            src, dst = piece(own), piece(near)
        sem = k if first else 8 + 8 * step + k
        return remote(src, dst, xy_send.at[sem], xy_recv.at[sem], dev)

    def swap(gran, row, n):
        h = n // 2
        return remote(
            pbuf.at[rows_at(row + (1 - core) * h, h)], crecv.at[rows_at(lax.div(row, 2), h)],
            ce_send.at[gran], ce_recv.at[gran], partner,
        )

    def rs_copy(gran, row, n, k):
        m = n // 8
        return remote(
            zsend.at[rows_at(lax.div(row, 2) + lax.rem(z + k, 4) * m, m)],
            zrecv.at[k - 1, rows_at(lax.div(row, 8), m)],
            rs_send.at[gran, k - 1], rs_recv.at[gran, k - 1], zpeer(k),
        )

    def ag_copy(gran, row, n, k):
        m = n // 8
        here = rbuf.at[rows_at(row + core * (n // 2) + z * m, m)]
        return remote(here, here, ag_send.at[gran, k - 1], ag_recv.at[gran, k - 1], zpeer(k))

    def ag_arrival(gran, row, n, k):
        m = n // 8
        there = rbuf.at[rows_at(row + core * (n // 2) + lax.rem(z + 4 - k, 4) * m, m)]
        return remote(there, there, ag_send.at[gran, k - 1], ag_recv.at[gran, k - 1], zpeer(k))

    def half_copy(gran, row, n, c):
        there = rbuf.at[rows_at(row + c * (n // 2), n // 2)]
        return remote(there, there, cf_send.at[gran], cf_recv.at[gran], partner)

    def multiply(gran, row, n):
        rows = rows_at(row, n)
        pbuf[rows, :] = jnp.dot(abuf[rows, :], bin_v[...], preferred_element_type=F32).astype(BF)
        swap(gran, row, n).start()

    def pair(gran, row, n):
        h = n // 2
        swap(gran, row, n).wait_recv()
        mine = pbuf[rows_at(row + core * h, h), :].astype(F32)
        theirs = crecv[rows_at(lax.div(row, 2), h), :].astype(F32)
        zsend[rows_at(lax.div(row, 2), h), :] = (mine + theirs).astype(BF)
        for k in (2, 1, 3):
            rs_copy(gran, row, n, k).start()

    def combine(gran, row, n):
        h, m = n // 2, n // 8
        total = pbuf[rows_at(row + core * h + z * m, m), :].astype(F32)
        total = total + crecv[rows_at(lax.div(row, 2) + z * m, m), :].astype(F32)
        for k in (1, 3, 2):
            rs_copy(gran, row, n, k).wait_recv()
            total = total + zrecv[k - 1, rows_at(lax.div(row, 8), m), :].astype(F32)
        rbuf[rows_at(row + core * h + z * m, m), :] = total.astype(BF)
        for k in (2, 1, 3):
            ag_copy(gran, row, n, k).start()

    def spread(gran, row, n):
        for k in (1, 3, 2):
            ag_arrival(gran, row, n, k).wait_recv()
        half_copy(gran, row, n, core).start()

    def finish(gran, row, n):
        half_copy(gran, row, n, 1 - core).wait_recv()

    def store(i, block, half):
        return pltpu.make_async_copy(
            rbuf.at[rows_at(i * HALF, HALF)],
            r_hbm.at[rows_at(block * TOK + half * HALF, HALF)],
            out_sem.at[i],
        )

    GH = FEAT // 2
    GQ = FEAT // 4

    def gg(phase, k):
        fwd = k % 4 >= 2
        minus = k % 2
        is_y = k >= 4
        buf = gy if is_y else gx
        if phase == 0:
            dev = ((yp, ym) if is_y else (xp, xm))[minus]
            if fwd:
                rows = pl.ds(GQ * minus, GQ)
                src, dst = buf.at[0, 1 + minus, rows], buf.at[0, 3, rows]
            else:
                src, dst = buf.at[0, 0], buf.at[0, 1 + minus]
        else:
            dev = ((xp, xm) if is_y else (yp, ym))[minus]
            if fwd:
                part = pl.ds(2 * minus, 2)
                src, dst = buf.at[1 + minus, part], buf.at[3, part]
            else:
                src, dst = buf.at[0], buf.at[1 + minus]
        sem = 8 * phase + k
        return remote(src, dst, gg_send.at[sem], gg_recv.at[sem], dev)

    def gr_swap():
        return remote(gpart.at[1 - core], gcrecv, gr_send.at[0], gr_recv.at[0], partner)

    def gr_copy(k):
        return remote(gzsend.at[lax.rem(z + k, 4)], gzrecv.at[k - 1], gr_send.at[k], gr_recv.at[k], zpeer(k))

    loads[0].wait()
    loads[1].wait()
    for half, i in ((0, 0), (1, 4)):
        g = gate_v[pl.ds(half * HALF, HALF), :].astype(F32)
        u = up_v[pl.ds(half * HALF, HALF), :].astype(F32)
        abuf[pl.ds(i * HALF, HALF), :] = (g / (1.0 + jnp.exp(-g)) * u).astype(BF)
        for k in (0, 1):
            xy(-1, 4 * half + k).start()

    loads[2].wait()
    loads[3].wait()

    def rotate(c, carry):
        cols = pl.ds(pl.multiple_of(c * FEAT, 128), FEAT)
        gpart[lax.rem(c, 2), lax.div(c, 2)] = jnp.dot(grad_v[...], bout_v[:, cols], preferred_element_type=F32)
        return carry

    lax.fori_loop(0, NT, rotate, 0)
    gr_swap().start()
    gr_swap().wait_recv()
    for k in (2, 1, 3):
        there = lax.rem(z + k, 4)
        gzsend[there] = (gpart[core, there] + gcrecv[there]).astype(BF)
        gr_copy(k).start()
    loads[4].wait()

    for k in (0, 1, 4, 5):
        xy(-1, k).wait_recv()
        xy(-1, k + 2).start()
    for k in (0, 1, 4, 5):
        xy(0, k).start()

    share = gpart[core, z] + gcrecv[z]
    for k in (1, 3, 2):
        gr_copy(k).wait_recv()
        share = share + gzrecv[k - 1].astype(F32)
    share = share.T.astype(BF)
    gx[0, 0] = share[:GH]
    gy[0, 0] = share[GH:]

    for k in (2, 3, 6, 7):
        xy(-1, k).wait_recv()
    for k in (0, 1, 4, 5):
        xy(1, k).start()

    def own(stage):
        lax.fori_loop(0, 2, lambda g, c: (stage(g, g * 256, 256), c)[1], 0)

    own(multiply)
    own(pair)
    own(combine)

    def step(j, carry):
        row = OWN * HALF + j * (PER * HALF)
        near = (2 + 2 * j, row, 256)
        far = (3 + 2 * j, row + 256, 128)
        old = (1 + 2 * j, row - 128, 128)
        later = pl.when(j > 0)
        for k in (0, 1, 4, 5):
            xy(j, k).wait_recv()
            xy(j, k + 2).start()

        @pl.when(j < 2)
        def _():
            for k in (0, 1, 4, 5):
                xy(j + 2, k).start()

        @pl.when(j == 0)
        def _():
            for k in (0, 1, 4, 5):
                gg(0, k).start()

        @pl.when(j == 1)
        def _():
            for k in (0, 1, 4, 5):
                gg(0, k).wait_recv()
                gg(0, k + 2).start()

        @pl.when(j == 3)
        def _():
            for k in (2, 3, 6, 7):
                gg(0, k).wait_recv()
            for k in (0, 1, 4, 5):
                gg(1, k).start()

        multiply(*near)

        @pl.when(j == 0)
        def _():
            own(spread)

        @later
        def _():
            combine(*old)

        pair(*near)

        @later
        def _():
            spread(*old)

        combine(*near)
        for k in (2, 3, 6, 7):
            xy(j, k).wait_recv()
        multiply(*far)
        spread(*near)
        pair(*far)
        return carry

    lax.fori_loop(0, STEPS, step, 0)
    last = (9, 2048 - 128, 128)
    combine(*last)

    OFF = (0, -1, 1, 2)
    outs = []

    def put(c):
        c.start()
        outs.append(c)

    def granules():
        for g in range(10):
            yield (g, 256 * g, 256) if g < 2 else (g, 512 + 384 * ((g - 2) // 2) + 256 * (g % 2), 128 if g % 2 else 256)

    every = list(granules())
    for g in every[:9]:
        finish(*g)
    for i in range(4):
        put(store(i, block_of(OFF[i], 0), 0))
        put(store(4 + i, block_of(0, OFF[i]), 1))
    for j in range(STEPS):
        b = OWN + PER * j
        put(store(b, block_of(OFF[j], -1), 0))
        put(store(b + 1, block_of(OFF[j], 1), 0))
        put(store(b + 2, block_of(-1, OFF[j]), 1))
        put(store(b + 3, block_of(1, OFF[j]), 1))
        if j < 3:
            put(store(b + 4, block_of(OFF[j], 2), 0))
            put(store(b + 5, block_of(2, OFF[j]), 1))
    spread(*last)
    for k in (0, 1, 4, 5):
        gg(1, k).wait_recv()
        gg(1, k + 2).start()

    def put_gradient(a):
        for b in range(4):
            for buf, half, dx, dy in ((gx, 0, OFF[b], OFF[a]), (gy, 1, OFF[a], OFF[b])):
                put(
                    pltpu.make_async_copy(
                        buf.at[a, b],
                        gt_hbm.at[block_of(dx, dy), pl.ds(half * GH, GH)],
                        out_sem.at[32 + half * 16 + 4 * a + b],
                    )
                )

    for a in range(3):
        put_gradient(a)
    finish(*last)
    put(store(30, block_of(2, 2), 0))
    put(store(31, block_of(2, 2), 1))

    for k in range(8):
        xy(-1, k).wait_send()
        gg(0, k).wait_send()
    for j in range(STEPS):
        for k in range(8):
            xy(j, k).wait_send()
    gr_swap().wait_send()
    for k in (1, 2, 3):
        gr_copy(k).wait_send()
    for g in every:
        swap(*g).wait_send()
        half_copy(*g, core).wait_send()
        for k in (1, 2, 3):
            rs_copy(*g, k).wait_send()
            ag_copy(*g, k).wait_send()
    for k in (2, 3, 6, 7):
        gg(1, k).wait_recv()
    put_gradient(3)
    for k in range(8):
        gg(1, k).wait_send()
    for c in outs:
        c.wait()


def gather_call(gate, up, grad, basis_in, basis_out):
    vm = pltpu.VMEM
    dma = pltpu.SemaphoreType.DMA
    hbm = pl.BlockSpec(memory_space=pl.ANY)
    return pl.pallas_call(
        gather_kernel,
        out_shape=(
            jax.ShapeDtypeStruct((2048, COLS), BF),
            jax.ShapeDtypeStruct((16, FEAT, TOK), BF),
        ),
        in_specs=[hbm] * 5,
        out_specs=(hbm, hbm),
        scratch_shapes=[
            vm((TOK, HID), BF), vm((TOK, HID), BF), vm((TOK, FEAT), BF), vm((HID, COLS), BF), vm((FEAT, D), BF),
            vm((2048, HID), BF), vm((2048, COLS), BF), vm((1024, COLS), BF), vm((1024, COLS), BF),
            vm((3, 256, COLS), BF), vm((2048, COLS), BF),
            vm((2, 4, TOK, FEAT), F32), vm((4, TOK, FEAT), F32), vm((4, TOK, FEAT), BF), vm((3, TOK, FEAT), BF),
            vm((4, 4, FEAT // 2, TOK), BF), vm((4, 4, FEAT // 2, TOK), BF),
            dma((5,)), dma((40,)), dma((40,)), dma((10,)), dma((10,)), dma((10, 3)), dma((10, 3)),
            dma((10, 3)), dma((10, 3)), dma((10,)), dma((10,)),
            dma((4,)), dma((4,)), dma((16,)), dma((16,)), dma((64,)),
        ],
        compiler_params=pltpu.CompilerParams(
            collective_id=0, has_side_effects=True, vmem_limit_bytes=58 * 2**20
        ),
        name="rotate_gather",
    )(gate, up, grad, basis_in, basis_out)


KB = 256


def fit_kernel(lengths, r_ref, gt_ref, out_ref):
    out_ref[...] = jnp.zeros_like(out_ref)

    def add(s, begin):
        end = begin + lengths[s]
        first = lax.div(begin, KB)
        blocks = lax.div(end + KB - 1, KB) - first

        for n in (1, 2, 3):

            @pl.when(blocks == n)
            def _():
                row = pl.multiple_of(first * KB, KB)
                r = r_ref[pl.ds(row, n * KB), :]
                token = row + lax.broadcasted_iota(jnp.int32, r.shape, 0)
                r = jnp.where((token >= begin) & (token < end), r, jnp.zeros_like(r))
                g = jnp.concatenate([gt_ref[2 * first + i] for i in range(2 * n)], axis=1)
                p = jnp.dot(g, r, preferred_element_type=F32)
                out_ref[...] += p * p

        return end

    lax.fori_loop(0, 8, add, 0)
    out_ref[...] = out_ref[...] * 0.125


def fit_call(lengths, r, gt):
    whole = pl.BlockSpec(memory_space=pltpu.VMEM)
    return pl.pallas_call(
        fit_kernel,
        out_shape=jax.ShapeDtypeStruct((FEAT, COLS), F32),
        in_specs=[pl.BlockSpec(memory_space=pltpu.SMEM), whole, whole],
        out_specs=whole,
        compiler_params=pltpu.CompilerParams(vmem_limit_bytes=58 * 2**20),
        name="sequence_products",
    )(lengths, r, gt)


def shards(gate_pre, up_pre, out_grad, basis_in, basis_out, lengths):
    r, gt = gather_call(gate_pre, up_pre, out_grad, basis_in, basis_out)
    return fit_call(lengths, r, gt)


def solution(mesh):
    return jax.shard_map(
        shards,
        mesh=mesh,
        in_specs=(
            P(("batch", "grid"), "tensor"),
            P(("batch", "grid"), "tensor"),
            P(("batch", "grid"), "tensor"),
            P("tensor", ("batch", "grid")),
            P("tensor", None),
            P(),
        ),
        out_specs=P("tensor", ("batch", "grid")),
        check_vma=False,
    )
```

time: 140 us -> 129 us (0.921); the launches traced: 140 us -> 127 us
  Pallas kernels: 140 us -> 127 us
    pallas_call x1, Pallas kernels: 129 us -> 116 us  [gather_call(): pl.pallas_call(gather_kernel, out_shape=(jax.ShapeDtypeStruct((2048, COLS...]
where the time goes in v2:
time: 129 us; the launch traced here: 127 us
  Pallas kernels  127 us (98%)
    pallas_call x1, Pallas kernels, gather_call(): pl.pallas_call(gather_kernel, out_shape=(jax.ShapeDtypeStruct((2048, COLS...  116 us
    pallas_call x1, Pallas kernels, fit_call(): pl.pallas_call(fit_kernel, out_shape=jax.ShapeDtypeStruct((FEAT, COLS), F...  11.3 us

profile of v2, /device:TPU:1, one launch (start us, length us, event | category | flops | bytes accessed | tf_op | source)
XLA Modules:
  0.0 127.4 jit_solution(5046252550969319876)
XLA Ops:
  0.0 116.1 %rotate_gather.1 = (bf16[2048,896]{1,0:T(8,128)(2,1)}, bf16[16,640,128]{2,1,0:T(8,128)(2,1)}) custom-call(bf16[128,3456]{1,0:T(8,128)(2,1)} %gate_hbm.1, bf16[128,3456]{1,0:T(8,128)(2,1)} %up_hbm.1, bf16[128,640]{1,0:T(8,128)(2,1)} %grad_hbm.1, bf16[3456,896]{1,0:T(8,128)(2,1)} %bin_hbm.1, bf16[640,5120]{1,0:T(8,128)(2,1)} %bout_hbm.1), custom_call_target="tpu_custom_call" | custom-call | tf_op jit(solution)/shard_map/rotate_gather/pallas_call | solution.py:393
  116.1 11.3 %sequence_products.1 = f32[640,896]{1,0:T(8,128)} custom-call(s32[8]{0:T(128)} %lengths.1, bf16[2048,896]{1,0:T(8,128)(2,1)} %get-tuple-element.7.r_ref, bf16[16,640,128]{2,1,0:T(8,128)(2,1)} %get-tuple-element.8.gt_ref), custom_call_target="tpu_custom_call" | custom-call | tf_op jit(solution)/shard_map/sequence_products/pallas_call | solution.py:449

commit v3 on v2

v3 whole, which is shorter than its diff:
```python
import functools

import jax
import jax.numpy as jnp
from jax import lax
from jax.experimental import pallas as pl
from jax.experimental.pallas import tpu as pltpu
from jax.sharding import PartitionSpec as P

MESH = pl.DeviceIdType.MESH
BF = jnp.bfloat16
F32 = jnp.float32

TOK = 128
HALF = 64
QUART = 32
HID = 3456
COLS = 896
FEAT = 640
D = 5120
NT = 8
STEPS = 4
OWN = 8
PER = 6


def gather_kernel(
    gate_hbm, up_hbm, grad_hbm, bin_hbm, bout_hbm, r_hbm, gt_hbm,
    gate_v, up_v, grad_v, bin_v, bout_v,
    abuf, pbuf, crecv, zsend, zrecv, rbuf, gpart, gcrecv, gzrecv, gx, gy,
    load_sem, xy_send, xy_recv, ce_send, ce_recv, rs_send, rs_recv, ag_send, ag_recv, cf_send, cf_recv,
    gr_send, gr_recv, gg_send, gg_recv, out_sem,
):
    xl = lax.axis_index("batch")
    me = lax.axis_index("tensor")
    gi = lax.axis_index("grid")
    x = lax.div(gi, 4) * 2 + xl
    y = lax.rem(gi, 4)
    z = lax.div(me, 2)
    core = lax.rem(me, 2)

    def at(dx, dy):
        xx = lax.rem(x + (dx + 4), 4)
        yy = lax.rem(y + (dy + 4), 4)
        return (lax.rem(xx, 2), me, lax.div(xx, 2) * 4 + yy)

    def block_of(dx, dy):
        b, _, g = at(dx, dy)
        return b * 8 + g

    def zpeer(k):
        return (xl, lax.rem(z + k, 4) * 2 + core, gi)

    partner = (xl, z * 2 + 1 - core, gi)
    xp, xm, yp, ym = at(1, 0), at(-1, 0), at(0, 1), at(0, -1)

    loads = [
        pltpu.make_async_copy(s, d, load_sem.at[i])
        for i, (s, d) in enumerate(
            [(gate_hbm, gate_v), (up_hbm, up_v), (grad_hbm, grad_v), (bout_hbm, bout_v), (bin_hbm, bin_v)]
        )
    ]
    loads[0].start()
    loads[1].start()

    barrier = pltpu.get_barrier_semaphore()
    for dev in [xp, xm, yp, ym, partner, zpeer(1), zpeer(2), zpeer(3)]:
        pl.semaphore_signal(barrier, inc=1, device_id=dev, device_id_type=MESH)
    pl.semaphore_wait(barrier, 8)

    def remote(src, dst, ss, rs, dev):
        return pltpu.make_async_remote_copy(
            src_ref=src, dst_ref=dst, send_sem=ss, recv_sem=rs, device_id=dev, device_id_type=MESH
        )

    def rows_at(i, n):
        return pl.ds(pl.multiple_of(i, 16), n)

    def piece(i, off=0, n=HALF):
        return abuf.at[rows_at(i * HALF + off, n)]

    def xy(step, k):
        first = isinstance(step, int) and step < 0
        fwd = k % 4 >= 2
        minus = k % 2
        is_y = k >= 4
        if first:
            base = 4 if is_y else 0
            own, near, far = base, base + 1 + minus, base + 3
            dev = ((yp, ym) if is_y else (xp, xm))[minus]
        else:
            b = OWN + PER * step
            own = (4 if is_y else 0) + step
            near = b + (2 if is_y else 0) + minus
            far = b + 4 + (1 if is_y else 0)
            dev = ((xp, xm) if is_y else (yp, ym))[minus]
        if fwd:
            src, dst = piece(near, QUART * minus, QUART), piece(far, QUART * minus, QUART)
        else:
            src, dst = piece(own), piece(near)
        sem = k if first else 8 + 8 * step + k
        return remote(src, dst, xy_send.at[sem], xy_recv.at[sem], dev)

    def swap(gran, row, n):
        h = n // 2
        return remote(
            pbuf.at[rows_at(row + (1 - core) * h, h)], crecv.at[rows_at(lax.div(row, 2), h)],
            ce_send.at[gran], ce_recv.at[gran], partner,
        )

    def rs_copy(gran, row, n, k):
        m = n // 8
        return remote(
            zsend.at[rows_at(lax.div(row, 2) + lax.rem(z + k, 4) * m, m)],
            zrecv.at[k - 1, rows_at(lax.div(row, 8), m)],
            rs_send.at[gran, k - 1], rs_recv.at[gran, k - 1], zpeer(k),
        )

    def ag_copy(gran, row, n, k):
        m = n // 8
        here = rbuf.at[rows_at(row + core * (n // 2) + z * m, m)]
        return remote(here, here, ag_send.at[gran, k - 1], ag_recv.at[gran, k - 1], zpeer(k))

    def ag_arrival(gran, row, n, k):
        m = n // 8
        there = rbuf.at[rows_at(row + core * (n // 2) + lax.rem(z + 4 - k, 4) * m, m)]
        return remote(there, there, ag_send.at[gran, k - 1], ag_recv.at[gran, k - 1], zpeer(k))

    def half_copy(gran, row, n, c):
        there = rbuf.at[rows_at(row + c * (n // 2), n // 2)]
        return remote(there, there, cf_send.at[gran], cf_recv.at[gran], partner)

    def multiply(gran, row, n):
        rows = rows_at(row, n)
        pbuf[rows, :] = jnp.dot(abuf[rows, :], bin_v[...], preferred_element_type=F32)
        swap(gran, row, n).start()

    def pair(gran, row, n):
        h = n // 2
        swap(gran, row, n).wait_recv()
        mine = pbuf[rows_at(row + core * h, h), :]
        theirs = crecv[rows_at(lax.div(row, 2), h), :]
        zsend[rows_at(lax.div(row, 2), h), :] = (mine + theirs).astype(BF)
        for k in (2, 1, 3):
            rs_copy(gran, row, n, k).start()

    def combine(gran, row, n):
        h, m = n // 2, n // 8
        total = pbuf[rows_at(row + core * h + z * m, m), :] + crecv[rows_at(lax.div(row, 2) + z * m, m), :]
        for k in (1, 3, 2):
            rs_copy(gran, row, n, k).wait_recv()
            total = total + zrecv[k - 1, rows_at(lax.div(row, 8), m), :].astype(F32)
        rbuf[rows_at(row + core * h + z * m, m), :] = total.astype(BF)
        for k in (2, 1, 3):
            ag_copy(gran, row, n, k).start()

    def spread(gran, row, n):
        for k in (1, 3, 2):
            ag_arrival(gran, row, n, k).wait_recv()
        half_copy(gran, row, n, core).start()

    def finish(gran, row, n):
        half_copy(gran, row, n, 1 - core).wait_recv()

    def store(slot, row, n):
        rows = rows_at(row, n)
        return pltpu.make_async_copy(rbuf.at[rows], r_hbm.at[rows], out_sem.at[slot])

    def store_gradient(slot, half, first, n):
        part = pl.ds(first, n)
        return pltpu.make_async_copy((gx, gy)[half].at[part], gt_hbm.at[half, part], out_sem.at[slot])

    def sent(gran, row, n):
        swap(gran, row, n).wait_send()
        half_copy(gran, row, n, core).wait_send()
        for k in (1, 2, 3):
            rs_copy(gran, row, n, k).wait_send()
            ag_copy(gran, row, n, k).wait_send()

    GH = FEAT // 2
    GQ = FEAT // 4

    def gg(phase, k):
        fwd = k % 4 >= 2
        minus = k % 2
        is_y = k >= 4
        buf = gy if is_y else gx
        if phase == 0:
            dev = ((yp, ym) if is_y else (xp, xm))[minus]
            if fwd:
                rows = pl.ds(GQ * minus, GQ)
                src, dst = buf.at[0, 1 + minus, rows], buf.at[0, 3, rows]
            else:
                src, dst = buf.at[0, 0], buf.at[0, 1 + minus]
        else:
            dev = ((xp, xm) if is_y else (yp, ym))[minus]
            if fwd:
                one = 2 * (phase - 1) + minus
                src, dst = buf.at[1 + minus, one], buf.at[3, one]
            else:
                part = pl.ds(2 * (phase - 1), 2)
                src, dst = buf.at[0, part], buf.at[1 + minus, part]
        sem = 8 * phase + k
        return remote(src, dst, gg_send.at[sem], gg_recv.at[sem], dev)

    def gr_swap():
        return remote(gpart.at[1 - core], gcrecv, gr_send.at[0], gr_recv.at[0], partner)

    def gr_copy(k):
        return remote(gpart.at[core, lax.rem(z + k, 4)], gzrecv.at[k - 1], gr_send.at[k], gr_recv.at[k], zpeer(k))

    loads[0].wait()
    loads[1].wait()
    for half, i in ((0, 0), (1, 4)):
        g = gate_v[pl.ds(half * HALF, HALF), :].astype(F32)
        u = up_v[pl.ds(half * HALF, HALF), :].astype(F32)
        abuf[pl.ds(i * HALF, HALF), :] = (g / (1.0 + jnp.exp(-g)) * u).astype(BF)
        for k in (0, 1):
            xy(-1, 4 * half + k).start()
        if half == 0:
            for c in loads[2:]:
                c.start()

    loads[2].wait()
    loads[3].wait()

    def rotate(c, carry):
        cols = pl.ds(pl.multiple_of(c * FEAT, 128), FEAT)
        gpart[lax.rem(c, 2), lax.div(c, 2)] = jnp.dot(grad_v[...], bout_v[:, cols], preferred_element_type=F32)
        return carry

    lax.fori_loop(0, NT, rotate, 0)
    gr_swap().start()
    for k in (0, 1, 4, 5):
        xy(0, k).start()
    gr_swap().wait_recv()
    for k in (2, 1, 3):
        there = lax.rem(z + k, 4)
        gpart[core, there] = gpart[core, there] + gcrecv[there]
        gr_copy(k).start()
    loads[4].wait()

    for k in (0, 1, 4, 5):
        xy(-1, k).wait_recv()
        xy(-1, k + 2).start()
    for k in (0, 1, 4, 5):
        xy(1, k).start()

    def near_of(j):
        return (2 + 2 * j, OWN * HALF + j * (PER * HALF), 256)

    def far_of(j):
        return (3 + 2 * j, OWN * HALF + j * (PER * HALF) + 256, 128)

    own = ((0, 0, 256), (1, 256, 256))

    def step(j, carry):
        for k in (0, 1, 4, 5):
            xy(j, k).wait_recv()
            xy(j, k + 2).start()

        @pl.when(j < 2)
        def _():
            @pl.when(j == 1)
            def _():
                for k in (0, 1, 4, 5):
                    gg(0, k).start()

            for k in (0, 1, 4, 5):
                xy(j + 2, k).start()

        @pl.when(j == 2)
        def _():
            for k in (0, 1, 4, 5):
                gg(0, k).wait_recv()
                gg(0, k + 2).start()

        @pl.when(j == 3)
        def _():
            for k in (2, 3, 6, 7):
                gg(0, k).wait_recv()
            for phase in (1, 2):
                for k in (0, 1, 4, 5):
                    gg(phase, k).start()

        multiply(*near_of(j))

        @pl.when(j == 1)
        def _():
            for g in own:
                combine(*g)

        @pl.when(j > 1)
        def _():
            combine(*far_of(j - 2))

        @pl.when(j > 0)
        def _():
            spread(*near_of(j - 1))

        pair(*near_of(j))

        @pl.when(j == 0)
        def _():
            for k in (2, 3, 6, 7):
                xy(-1, k).wait_recv()
            lax.fori_loop(0, 2, lambda g, c: (multiply(g, g * 256, 256), c)[1], 0)
            for g in own:
                pair(*g)

        @pl.when(j > 0)
        def _():
            for k in (2, 3, 6, 7):
                xy(j - 1, k).wait_recv()
            multiply(*far_of(j - 1))
            pair(*far_of(j - 1))

        combine(*near_of(j))

        @pl.when(j == 0)
        def _():
            share = gpart[core, z] + gcrecv[z]
            for k in (1, 3, 2):
                gr_copy(k).wait_recv()
                share = share + gzrecv[k - 1]
            share = share.T.astype(BF)
            gx[0, 0] = share[:GH]
            gy[0, 0] = share[GH:]

        @pl.when(j == 1)
        def _():
            for g in own:
                spread(*g)
            for k in range(8):
                xy(-1, k).wait_send()
            gr_swap().wait_send()
            for k in (1, 2, 3):
                gr_copy(k).wait_send()

        @pl.when(j > 1)
        def _():
            spread(*far_of(j - 2))
            for k in range(8):
                xy(j - 2, k).wait_send()

        @pl.when(j == 2)
        def _():
            for g in own:
                finish(*g)
                sent(*g)
            store(0, 0, 512).start()

        @pl.when(j == 3)
        def _():
            for g in (near_of(0), far_of(0)):
                finish(*g)
                sent(*g)
            store(1, 512, 384).start()

        return carry

    lax.fori_loop(0, STEPS, step, 0)

    def forward(phase):
        for k in (0, 1, 4, 5):
            gg(phase, k).wait_recv()
            gg(phase, k + 2).start()

    for k in (2, 3, 6, 7):
        xy(3, k).wait_recv()
    multiply(*far_of(3))
    combine(*far_of(2))
    spread(*near_of(3))
    pair(*far_of(3))
    forward(1)
    for g in (near_of(1), far_of(1)):
        finish(*g)
    store(2, 512 + 384, 384).start()
    spread(*far_of(2))
    combine(*far_of(3))
    forward(2)
    for half in (0, 1):
        store_gradient(6 + half, half, 0, 3).start()
    for g in (near_of(2), far_of(2), near_of(3)):
        finish(*g)
    store(3, 512 + 768, 384 + 256).start()
    for g in (near_of(1), far_of(1), near_of(2)):
        sent(*g)
    for j in (2, 3):
        for k in range(8):
            xy(j, k).wait_send()
    for k in range(8):
        gg(0, k).wait_send()
    spread(*far_of(3))
    for g in (far_of(2), near_of(3)):
        sent(*g)
    for phase in (1, 2):
        for k in (2, 3, 6, 7):
            gg(phase, k).wait_recv()
    for half in (0, 1):
        store_gradient(8 + half, half, 3, 1).start()
    finish(*far_of(3))
    store(5, 2048 - 128, 128).start()
    sent(*far_of(3))
    for phase in (1, 2):
        for k in range(8):
            gg(phase, k).wait_send()
    store(0, 0, 512).wait()
    store(1, 512, 384).wait()
    store(2, 512 + 384, 384).wait()
    store(3, 512 + 768, 384 + 256).wait()
    store(5, 2048 - 128, 128).wait()
    for half in (0, 1):
        store_gradient(6 + half, half, 0, 3).wait()
        store_gradient(8 + half, half, 3, 1).wait()


def gather_call(gate, up, grad, basis_in, basis_out):
    vm = pltpu.VMEM
    dma = pltpu.SemaphoreType.DMA
    hbm = pl.BlockSpec(memory_space=pl.ANY)
    return pl.pallas_call(
        gather_kernel,
        out_shape=(
            jax.ShapeDtypeStruct((2048, COLS), BF),
            jax.ShapeDtypeStruct((2, 4, 4, FEAT // 2, TOK), BF),
        ),
        in_specs=[hbm] * 5,
        out_specs=(hbm, hbm),
        scratch_shapes=[
            vm((TOK, HID), BF), vm((TOK, HID), BF), vm((TOK, FEAT), BF), vm((HID, COLS), BF), vm((FEAT, D), BF),
            vm((2048, HID), BF), vm((2048, COLS), F32), vm((1024, COLS), F32), vm((1024, COLS), BF),
            vm((3, 256, COLS), BF), vm((2048, COLS), BF),
            vm((2, 4, TOK, FEAT), F32), vm((4, TOK, FEAT), F32), vm((3, TOK, FEAT), F32),
            vm((4, 4, FEAT // 2, TOK), BF), vm((4, 4, FEAT // 2, TOK), BF),
            dma((5,)), dma((40,)), dma((40,)), dma((10,)), dma((10,)), dma((10, 3)), dma((10, 3)),
            dma((10, 3)), dma((10, 3)), dma((10,)), dma((10,)),
            dma((4,)), dma((4,)), dma((24,)), dma((24,)), dma((10,)),
        ],
        compiler_params=pltpu.CompilerParams(
            collective_id=0, has_side_effects=True, vmem_limit_bytes=58 * 2**20
        ),
        name="rotate_gather",
    )(gate, up, grad, basis_in, basis_out)


KB = 256
NB = 896


def fit_kernel(lengths, r_ref, gt_ref, out_ref):
    gi = lax.axis_index("grid")
    x = lax.div(gi, 4) * 2 + lax.axis_index("batch")
    y = lax.rem(gi, 4)

    def code(there, here):
        d = lax.rem(there - here + 4, 4)
        return jnp.where(d == 0, 0, jnp.where(d == 3, 1, d + 1))

    def codes(block):
        bx = lax.rem(lax.div(block, 4), 2) * 2 + lax.div(block, 8)
        return code(bx, x), code(lax.rem(block, 4), y)

    def rows_of(cx, cy, half):
        a, b = (cx, cy) if half == 0 else (cy, cx)
        near = jnp.where(b == 3, 4 + half, b - 1 + 2 * half)
        i = jnp.where(b == 0, a + 4 * half, OWN + PER * a + near)
        return r_ref[pl.ds(pl.multiple_of(i * HALF, HALF), HALF), :]

    out_ref[...] = jnp.zeros_like(out_ref)

    def add(s, begin):
        end = begin + lengths[s]
        first = lax.div(begin, KB)
        blocks = lax.div(end + KB - 1, KB) - first

        for n in (1, 2, 3):

            @pl.when(blocks == n)
            def _():
                rs, gs = [], []
                for i in range(2 * n):
                    cx, cy = codes(2 * first + i)
                    rs += [rows_of(cx, cy, 0), rows_of(cx, cy, 1)]
                    gs.append(jnp.concatenate([gt_ref[0, cy, cx], gt_ref[1, cx, cy]], axis=0))
                r = jnp.concatenate(rs, axis=0)
                token = first * KB + lax.broadcasted_iota(jnp.int32, r.shape, 0)
                r = jnp.where((token >= begin) & (token < end), r, jnp.zeros_like(r))
                p = jnp.dot(jnp.concatenate(gs, axis=1), r, preferred_element_type=F32)
                out_ref[...] += p * p

        return end

    lax.fori_loop(0, 8, add, 0)
    out_ref[...] = out_ref[...] * 0.125


def fit_call(lengths, r, gt):
    return pl.pallas_call(
        fit_kernel,
        grid=(pl.cdiv(COLS, NB),),
        out_shape=jax.ShapeDtypeStruct((FEAT, COLS), F32),
        in_specs=[
            pl.BlockSpec(memory_space=pltpu.SMEM),
            pl.BlockSpec((2048, NB), lambda i: (0, i)),
            pl.BlockSpec(memory_space=pltpu.VMEM),
        ],
        out_specs=pl.BlockSpec((FEAT, NB), lambda i: (0, i)),
        compiler_params=pltpu.CompilerParams(vmem_limit_bytes=58 * 2**20),
        name="sequence_products",
    )(lengths, r, gt)


def shards(gate_pre, up_pre, out_grad, basis_in, basis_out, lengths):
    r, gt = gather_call(gate_pre, up_pre, out_grad, basis_in, basis_out)
    return fit_call(lengths, r, gt)


def solution(mesh):
    return jax.shard_map(
        shards,
        mesh=mesh,
        in_specs=(
            P(("batch", "grid"), "tensor"),
            P(("batch", "grid"), "tensor"),
            P(("batch", "grid"), "tensor"),
            P("tensor", ("batch", "grid")),
            P("tensor", None),
            P(),
        ),
        out_specs=P("tensor", ("batch", "grid")),
        check_vma=False,
    )
```

time: 129 us -> 117 us (0.907); the launches traced: 127 us -> 117 us
  Pallas kernels: 127 us -> 117 us
    pallas_call x1, Pallas kernels: 116 us -> 106 us  [gather_call(): pl.pallas_call(gather_kernel, out_shape=(jax.ShapeDtypeStruct((2048, COLS...]
where the time goes in v3:
time: 117 us
  Pallas kernels  117 us (100%)
    pallas_call x1, Pallas kernels, gather_call(): pl.pallas_call(gather_kernel, out_shape=(jax.ShapeDtypeStruct((2048, COLS...  106 us
    pallas_call x1, Pallas kernels, fit_call(): pl.pallas_call(fit_kernel, grid=(pl.cdiv(COLS, NB),), out_shape=jax.Shape...  11.5 us

profile of v3, /device:TPU:1, one launch (start us, length us, event | category | flops | bytes accessed | tf_op | source)
XLA Modules:
  0.0 117.0 jit_solution(11413038960187140208)
XLA Ops:
  0.0 105.6 %rotate_gather.1 = (bf16[2048,896]{1,0:T(8,128)(2,1)}, bf16[2,4,4,320,128]{4,3,2,1,0:T(8,128)(2,1)}) custom-call(bf16[128,3456]{1,0:T(8,128)(2,1)} %gate_hbm.1, bf16[128,3456]{1,0:T(8,128)(2,1)} %up_hbm.1, bf16[128,640]{1,0:T(8,128)(2,1)} %grad_hbm.1, bf16[3456,896]{1,0:T(8,128)(2,1)} %bin_hbm.1, bf16[640,5120]{1,0:T(8,128)(2,1)} %bout_hbm.1), custom_call_target="tpu_custom_call" | custom-call | tf_op jit(solution)/shard_map/rotate_gather/pallas_call | solution.py:422
  105.6 11.5 %sequence_products.1 = f32[640,896]{1,0:T(8,128)} custom-call(s32[8]{0:T(128)} %lengths.1, bf16[2048,896]{1,0:T(8,128)(2,1)} %get-tuple-element.7.r_ref, bf16[2,4,4,320,128]{4,3,2,1,0:T(8,128)(2,1)} %get-tuple-element.8.gt_ref), custom_call_target="tpu_custom_call" | custom-call | tf_op jit(solution)/shard_map/sequence_products/pallas_call | solution.py:499

commit v4 on v3

--- a/solution.py
+++ b/solution.py
@@ -79,7 +79,7 @@
     def piece(i, off=0, n=HALF):
         return abuf.at[rows_at(i * HALF + off, n)]
 
-    def xy(step, k):
+    def xy(step, k, part=0):
         first = isinstance(step, int) and step < 0
         fwd = k % 4 >= 2
         minus = k % 2
@@ -96,9 +96,11 @@
             dev = ((xp, xm) if is_y else (yp, ym))[minus]
         if fwd:
             src, dst = piece(near, QUART * minus, QUART), piece(far, QUART * minus, QUART)
+        elif first:
+            src, dst = piece(own, QUART * part, QUART), piece(near, QUART * part, QUART)
         else:
             src, dst = piece(own), piece(near)
-        sem = k if first else 8 + 8 * step + k
+        sem = (k + 40 * part if first else 8 + 8 * step + k)
         return remote(src, dst, xy_send.at[sem], xy_recv.at[sem], dev)
 
     def swap(gran, row, n):
@@ -162,13 +164,31 @@
     def finish(gran, row, n):
         half_copy(gran, row, n, 1 - core).wait_recv()
 
-    def store(slot, row, n):
-        rows = rows_at(row, n)
-        return pltpu.make_async_copy(rbuf.at[rows], r_hbm.at[rows], out_sem.at[slot])
-
-    def store_gradient(slot, half, first, n):
-        part = pl.ds(first, n)
-        return pltpu.make_async_copy((gx, gy)[half].at[part], gt_hbm.at[half, part], out_sem.at[slot])
+    def store(i, cx, cy, half):
+        return pltpu.make_async_copy(
+            rbuf.at[rows_at(i * HALF, HALF)], r_hbm.at[cx, cy, pl.ds(half * HALF, HALF)], out_sem.at[i]
+        )
+
+    def store_own():
+        return [store(i, i, 0, 0) for i in range(4)] + [store(4 + i, 0, i, 1) for i in range(4)]
+
+    def store_near(j):
+        b = OWN + PER * j
+        return [store(b, j, 1, 0), store(b + 1, j, 2, 0), store(b + 2, 1, j, 1), store(b + 3, 2, j, 1)]
+
+    def store_far(j):
+        b = OWN + PER * j
+        return [store(b + 4, j, 3, 0), store(b + 5, 3, j, 1)]
+
+    def store_gradient(i):
+        return [
+            pltpu.make_async_copy(gx.at[i], gt_hbm.at[:, i, pl.ds(0, GH)], out_sem.at[32 + i]),
+            pltpu.make_async_copy(gy.at[i], gt_hbm.at[i, :, pl.ds(GH, GH)], out_sem.at[36 + i]),
+        ]
+
+    def start(copies):
+        for c in copies:
+            c.start()
 
     def sent(gran, row, n):
         swap(gran, row, n).wait_send()
@@ -211,15 +231,17 @@
 
     loads[0].wait()
     loads[1].wait()
-    for half, i in ((0, 0), (1, 4)):
-        g = gate_v[pl.ds(half * HALF, HALF), :].astype(F32)
-        u = up_v[pl.ds(half * HALF, HALF), :].astype(F32)
-        abuf[pl.ds(i * HALF, HALF), :] = (g / (1.0 + jnp.exp(-g)) * u).astype(BF)
-        for k in (0, 1):
-            xy(-1, 4 * half + k).start()
-        if half == 0:
-            for c in loads[2:]:
-                c.start()
+    for part in (0, 1):
+        for half, i in ((0, 0), (1, 4)):
+            rows = pl.ds(half * HALF + part * QUART, QUART)
+            g = gate_v[rows, :].astype(F32)
+            u = up_v[rows, :].astype(F32)
+            abuf[pl.ds(i * HALF + part * QUART, QUART), :] = (g / (1.0 + jnp.exp(-g)) * u).astype(BF)
+            for k in (0, 1):
+                xy(-1, 4 * half + k, part).start()
+            if part == 0 and half == 1:
+                for c in loads[2:]:
+                    c.start()
 
     loads[2].wait()
     loads[3].wait()
@@ -241,7 +263,8 @@
     loads[4].wait()
 
     for k in (0, 1, 4, 5):
-        xy(-1, k).wait_recv()
+        for part in (0, 1):
+            xy(-1, k, part).wait_recv()
         xy(-1, k + 2).start()
     for k in (0, 1, 4, 5):
         xy(1, k).start()
@@ -333,6 +356,8 @@
                 spread(*g)
             for k in range(8):
                 xy(-1, k).wait_send()
+            for k in (0, 1, 4, 5):
+                xy(-1, k, 1).wait_send()
             gr_swap().wait_send()
             for k in (1, 2, 3):
                 gr_copy(k).wait_send()
@@ -348,14 +373,14 @@
             for g in own:
                 finish(*g)
                 sent(*g)
-            store(0, 0, 512).start()
+            start(store_own())
 
         @pl.when(j == 3)
         def _():
             for g in (near_of(0), far_of(0)):
                 finish(*g)
                 sent(*g)
-            store(1, 512, 384).start()
+            start(store_near(0) + store_far(0))
 
         return carry
 
@@ -369,50 +394,45 @@
     for k in (2, 3, 6, 7):
         xy(3, k).wait_recv()
     multiply(*far_of(3))
+    pair(*far_of(3))
     combine(*far_of(2))
+    forward(1)
     spread(*near_of(3))
-    pair(*far_of(3))
-    forward(1)
-    for g in (near_of(1), far_of(1)):
-        finish(*g)
-    store(2, 512 + 384, 384).start()
-    spread(*far_of(2))
     combine(*far_of(3))
     forward(2)
-    for half in (0, 1):
-        store_gradient(6 + half, half, 0, 3).start()
-    for g in (near_of(2), far_of(2), near_of(3)):
+    spread(*far_of(2))
+    start(store_gradient(1) + store_gradient(2))
+    for g in (far_of(2), near_of(3)):
         finish(*g)
-    store(3, 512 + 768, 384 + 256).start()
-    for g in (near_of(1), far_of(1), near_of(2)):
+    start(store_far(2) + store_near(3))
+    for g in (near_of(1), near_of(2)):
+        finish(*g)
+    start(store_near(1) + store_near(2))
+    spread(*far_of(3))
+    finish(*far_of(1))
+    start(store_far(1) + store_gradient(0))
+    for g in (near_of(1), far_of(1), near_of(2), far_of(2), near_of(3)):
         sent(*g)
     for j in (2, 3):
         for k in range(8):
             xy(j, k).wait_send()
     for k in range(8):
         gg(0, k).wait_send()
-    spread(*far_of(3))
-    for g in (far_of(2), near_of(3)):
-        sent(*g)
     for phase in (1, 2):
         for k in (2, 3, 6, 7):
             gg(phase, k).wait_recv()
-    for half in (0, 1):
-        store_gradient(8 + half, half, 3, 1).start()
+    start(store_gradient(3))
     finish(*far_of(3))
-    store(5, 2048 - 128, 128).start()
-    sent(*far_of(3))
+    start(store_far(3))
     for phase in (1, 2):
         for k in range(8):
             gg(phase, k).wait_send()
-    store(0, 0, 512).wait()
-    store(1, 512, 384).wait()
-    store(2, 512 + 384, 384).wait()
-    store(3, 512 + 768, 384 + 256).wait()
-    store(5, 2048 - 128, 128).wait()
-    for half in (0, 1):
-        store_gradient(6 + half, half, 0, 3).wait()
-        store_gradient(8 + half, half, 3, 1).wait()
+    sent(*far_of(3))
+    done = store_own()
+    for j in range(STEPS):
+        done += store_near(j) + store_far(j) + store_gradient(j)
+    for c in done:
+        c.wait()
 
 
 def gather_call(gate, up, grad, basis_in, basis_out):
@@ -422,8 +442,8 @@
     return pl.pallas_call(
         gather_kernel,
         out_shape=(
-            jax.ShapeDtypeStruct((2048, COLS), BF),
-            jax.ShapeDtypeStruct((2, 4, 4, FEAT // 2, TOK), BF),
+            jax.ShapeDtypeStruct((4, 4, TOK, COLS), BF),
+            jax.ShapeDtypeStruct((4, 4, FEAT, TOK), BF),
         ),
         in_specs=[hbm] * 5,
         out_specs=(hbm, hbm),
@@ -433,9 +453,9 @@
             vm((3, 256, COLS), BF), vm((2048, COLS), BF),
             vm((2, 4, TOK, FEAT), F32), vm((4, TOK, FEAT), F32), vm((3, TOK, FEAT), F32),
             vm((4, 4, FEAT // 2, TOK), BF), vm((4, 4, FEAT // 2, TOK), BF),
-            dma((5,)), dma((40,)), dma((40,)), dma((10,)), dma((10,)), dma((10, 3)), dma((10, 3)),
+            dma((5,)), dma((48,)), dma((48,)), dma((10,)), dma((10,)), dma((10, 3)), dma((10, 3)),
             dma((10, 3)), dma((10, 3)), dma((10,)), dma((10,)),
-            dma((4,)), dma((4,)), dma((24,)), dma((24,)), dma((10,)),
+            dma((4,)), dma((4,)), dma((24,)), dma((24,)), dma((40,)),
         ],
         compiler_params=pltpu.CompilerParams(
             collective_id=0, has_side_effects=True, vmem_limit_bytes=58 * 2**20
@@ -444,11 +464,11 @@
     )(gate, up, grad, basis_in, basis_out)
 
 
-KB = 256
-NB = 896
-
-
-def fit_kernel(lengths, r_ref, gt_ref, out_ref):
+KB = 128
+CUTS = ((0, 256), (256, 256), (512, 256), (768, 128))
+
+
+def fit_kernel(lengths, r_hbm, gt_hbm, out_hbm, r_ref, g_ref, acc, in_sem, out_sem):
     gi = lax.axis_index("grid")
     x = lax.div(gi, 4) * 2 + lax.axis_index("batch")
     y = lax.rem(gi, 4)
@@ -457,55 +477,79 @@
         d = lax.rem(there - here + 4, 4)
         return jnp.where(d == 0, 0, jnp.where(d == 3, 1, d + 1))
 
-    def codes(block):
-        bx = lax.rem(lax.div(block, 4), 2) * 2 + lax.div(block, 8)
-        return code(bx, x), code(lax.rem(block, 4), y)
-
-    def rows_of(cx, cy, half):
-        a, b = (cx, cy) if half == 0 else (cy, cx)
-        near = jnp.where(b == 3, 4 + half, b - 1 + 2 * half)
-        i = jnp.where(b == 0, a + 4 * half, OWN + PER * a + near)
-        return r_ref[pl.ds(pl.multiple_of(i * HALF, HALF), HALF), :]
-
-    out_ref[...] = jnp.zeros_like(out_ref)
+    def load(quarter):
+        cx = code(lax.rem(quarter, 2) * 2 + lax.div(quarter, 2), x)
+        return (
+            pltpu.make_async_copy(r_hbm.at[cx], r_ref.at[quarter], in_sem.at[quarter, 0]),
+            pltpu.make_async_copy(gt_hbm.at[cx], g_ref.at[quarter], in_sem.at[quarter, 1]),
+        )
+
+    for quarter in range(4):
+        for c in load(quarter):
+            c.start()
+    acc[...] = jnp.zeros_like(acc)
+
+    def results(c):
+        cols = pl.ds(*CUTS[c])
+        return pltpu.make_async_copy(acc.at[:, cols], out_hbm.at[:, cols], out_sem.at[c])
 
     def add(s, begin):
         end = begin + lengths[s]
         first = lax.div(begin, KB)
         blocks = lax.div(end + KB - 1, KB) - first
 
-        for n in (1, 2, 3):
-
-            @pl.when(blocks == n)
-            def _():
+        @pl.when(s < 4)
+        def _():
+            for c in load(s):
+                c.wait()
+
+        for n in range(1, 2 + 512 // KB):
+
+            def factors():
                 rs, gs = [], []
-                for i in range(2 * n):
-                    cx, cy = codes(2 * first + i)
-                    rs += [rows_of(cx, cy, 0), rows_of(cx, cy, 1)]
-                    gs.append(jnp.concatenate([gt_ref[0, cy, cx], gt_ref[1, cx, cy]], axis=0))
+                for i in range(n * KB // 128):
+                    block = first * (KB // 128) + i
+                    quarter, cy = lax.div(block, 4), code(lax.rem(block, 4), y)
+                    rs.append(r_ref[quarter, cy])
+                    gs.append(g_ref[quarter, cy])
                 r = jnp.concatenate(rs, axis=0)
                 token = first * KB + lax.broadcasted_iota(jnp.int32, r.shape, 0)
                 r = jnp.where((token >= begin) & (token < end), r, jnp.zeros_like(r))
-                p = jnp.dot(jnp.concatenate(gs, axis=1), r, preferred_element_type=F32)
-                out_ref[...] += p * p
+                return jnp.concatenate(gs, axis=1), r
+
+            @pl.when((blocks == n) & (s < 7))
+            def _():
+                g, r = factors()
+                p = jnp.dot(g, r, preferred_element_type=F32)
+                acc[...] += p * p
+
+            @pl.when((blocks == n) & (s == 7))
+            def _():
+                g, r = factors()
+                for c, (at, wide) in enumerate(CUTS):
+                    cols = pl.ds(at, wide)
+                    p = jnp.dot(g, r[:, at : at + wide], preferred_element_type=F32)
+                    acc[:, cols] = (acc[:, cols] + p * p) * 0.125
+                    results(c).start()
 
         return end
 
     lax.fori_loop(0, 8, add, 0)
-    out_ref[...] = out_ref[...] * 0.125
+    for c in range(len(CUTS)):
+        results(c).wait()
 
 
 def fit_call(lengths, r, gt):
+    hbm = pl.BlockSpec(memory_space=pl.ANY)
     return pl.pallas_call(
         fit_kernel,
-        grid=(pl.cdiv(COLS, NB),),
         out_shape=jax.ShapeDtypeStruct((FEAT, COLS), F32),
-        in_specs=[
-            pl.BlockSpec(memory_space=pltpu.SMEM),
-            pl.BlockSpec((2048, NB), lambda i: (0, i)),
-            pl.BlockSpec(memory_space=pltpu.VMEM),
+        in_specs=[pl.BlockSpec(memory_space=pltpu.SMEM), hbm, hbm],
+        out_specs=hbm,
+        scratch_shapes=[
+            pltpu.VMEM((4, 4, 128, COLS), BF), pltpu.VMEM((4, 4, FEAT, 128), BF), pltpu.VMEM((FEAT, COLS), F32),
+            pltpu.SemaphoreType.DMA((4, 2)), pltpu.SemaphoreType.DMA((4,)),
         ],
-        out_specs=pl.BlockSpec((FEAT, NB), lambda i: (0, i)),
         compiler_params=pltpu.CompilerParams(vmem_limit_bytes=58 * 2**20),
         name="sequence_products",
     )(lengths, r, gt)

time: 117 us -> 114 us (0.974)
  Pallas kernels: 117 us -> 113 us
    pallas_call x2, Pallas kernels: 117 us -> 113 us  [the longest x1 104 us: gather_call(): pl.pallas_call(gather_kernel, out_shape=(jax.ShapeDtypeStruct((4, 4, TOK,...]
where the time goes in v4:
time: 114 us; the launch traced here: 113 us
  Pallas kernels  113 us (99%)
    pallas_call x1, Pallas kernels, gather_call(): pl.pallas_call(gather_kernel, out_shape=(jax.ShapeDtypeStruct((4, 4, TOK,...  104 us
    pallas_call x1, Pallas kernels, fit_call(): pl.pallas_call(fit_kernel, out_shape=jax.ShapeDtypeStruct((FEAT, COLS), F...  9.74 us

profile of v4, /device:TPU:1, one launch (start us, length us, event | category | flops | bytes accessed | tf_op | source)
XLA Modules:
  0.0 113.5 jit_solution(408161312484932060)
XLA Ops:
  0.0 103.6 %rotate_gather.1 = (bf16[4,4,128,896]{3,2,1,0:T(8,128)(2,1)}, bf16[4,4,640,128]{3,2,1,0:T(8,128)(2,1)}) custom-call(bf16[128,3456]{1,0:T(8,128)(2,1)} %gate_hbm.1, bf16[128,3456]{1,0:T(8,128)(2,1)} %up_hbm.1, bf16[128,640]{1,0:T(8,128)(2,1)} %grad_hbm.1, bf16[3456,896]{1,0:T(8,128)(2,1)} %bin_hbm.1, bf16[640,5120]{1,0:T(8,128)(2,1)} %bout_hbm.1), custom_call_target="tpu_custom_call" | custom-call | tf_op jit(solution)/shard_map/rotate_gather/pallas_call | solution.py:442
  103.6 9.7 %sequence_products.1 = f32[640,896]{1,0:T(8,128)} custom-call(s32[8]{0:T(128)} %lengths.1, bf16[4,4,128,896]{3,2,1,0:T(8,128)(2,1)} %get-tuple-element.7.r_hbm, bf16[4,4,640,128]{3,2,1,0:T(8,128)(2,1)} %get-tuple-element.8.gt_hbm), custom_call_target="tpu_custom_call" | custom-call | tf_op jit(solution)/shard_map/sequence_products/pallas_call | solution.py:544

commit v5 on v4

--- a/solution.py
+++ b/solution.py
@@ -277,34 +277,30 @@
 
     own = ((0, 0, 256), (1, 256, 256))
 
-    def step(j, carry):
+    def pass_on(j):
         for k in (0, 1, 4, 5):
             xy(j, k).wait_recv()
             xy(j, k + 2).start()
 
         @pl.when(j < 2)
         def _():
-            @pl.when(j == 1)
-            def _():
-                for k in (0, 1, 4, 5):
-                    gg(0, k).start()
-
             for k in (0, 1, 4, 5):
                 xy(j + 2, k).start()
 
         @pl.when(j == 2)
+        def _():
+            for k in (0, 1, 4, 5):
+                gg(0, k).start()
+
+        @pl.when(j == 3)
         def _():
             for k in (0, 1, 4, 5):
                 gg(0, k).wait_recv()
                 gg(0, k + 2).start()
-
-        @pl.when(j == 3)
-        def _():
-            for k in (2, 3, 6, 7):
-                gg(0, k).wait_recv()
-            for phase in (1, 2):
-                for k in (0, 1, 4, 5):
-                    gg(phase, k).start()
+                gg(1, k).start()
+
+    def step(j, carry):
+        pass_on(j)
 
         multiply(*near_of(j))
 
@@ -394,6 +390,10 @@
     for k in (2, 3, 6, 7):
         xy(3, k).wait_recv()
     multiply(*far_of(3))
+    for k in (2, 3, 6, 7):
+        gg(0, k).wait_recv()
+    for k in (0, 1, 4, 5):
+        gg(2, k).start()
     pair(*far_of(3))
     combine(*far_of(2))
     forward(1)

time: 114 us -> 113 us (level)
  no operation moved by 1% of the time
where the time goes in v5:
time: 113 us; the launch traced here: 112 us
  Pallas kernels  112 us (99%)
    pallas_call x1, Pallas kernels, gather_call(): pl.pallas_call(gather_kernel, out_shape=(jax.ShapeDtypeStruct((4, 4, TOK,...  103 us
    pallas_call x1, Pallas kernels, fit_call(): pl.pallas_call(fit_kernel, out_shape=jax.ShapeDtypeStruct((FEAT, COLS), F...  9.49 us

profile of v5, /device:TPU:1, one launch (start us, length us, event | category | flops | bytes accessed | tf_op | source)
XLA Modules:
  0.0 112.4 jit_solution(17293630122482476927)
XLA Ops:
  0.0 102.7 %rotate_gather.1 = (bf16[4,4,128,896]{3,2,1,0:T(8,128)(2,1)}, bf16[4,4,640,128]{3,2,1,0:T(8,128)(2,1)}) custom-call(bf16[128,3456]{1,0:T(8,128)(2,1)} %gate_hbm.1, bf16[128,3456]{1,0:T(8,128)(2,1)} %up_hbm.1, bf16[128,640]{1,0:T(8,128)(2,1)} %grad_hbm.1, bf16[3456,896]{1,0:T(8,128)(2,1)} %bin_hbm.1, bf16[640,5120]{1,0:T(8,128)(2,1)} %bout_hbm.1), custom_call_target="tpu_custom_call" | custom-call | tf_op jit(solution)/shard_map/rotate_gather/pallas_call | solution.py:442
  102.7 9.5 %sequence_products.1 = f32[640,896]{1,0:T(8,128)} custom-call(s32[8]{0:T(128)} %lengths.1, bf16[4,4,128,896]{3,2,1,0:T(8,128)(2,1)} %get-tuple-element.7.r_hbm, bf16[4,4,640,128]{3,2,1,0:T(8,128)(2,1)} %get-tuple-element.8.gt_hbm), custom_call_target="tpu_custom_call" | custom-call | tf_op jit(solution)/shard_map/sequence_products/pallas_call | solution.py:544

commit v6 on v5

--- a/solution.py
+++ b/solution.py
@@ -418,6 +418,11 @@
             xy(j, k).wait_send()
     for k in range(8):
         gg(0, k).wait_send()
+    early = store_own() + store_near(3)
+    for j in range(3):
+        early += store_near(j) + store_far(j) + store_gradient(j)
+    for c in early:
+        c.wait()
     for phase in (1, 2):
         for k in (2, 3, 6, 7):
             gg(phase, k).wait_recv()
@@ -428,10 +433,7 @@
         for k in range(8):
             gg(phase, k).wait_send()
     sent(*far_of(3))
-    done = store_own()
-    for j in range(STEPS):
-        done += store_near(j) + store_far(j) + store_gradient(j)
-    for c in done:
+    for c in store_gradient(3) + store_far(3):
         c.wait()
 
 

time: 113 us -> 112 us (level)
  no operation moved by 1% of the time
where the time goes in v6:
time: 112 us
  Pallas kernels  112 us (100%)
    pallas_call x1, Pallas kernels, gather_call(): pl.pallas_call(gather_kernel, out_shape=(jax.ShapeDtypeStruct((4, 4, TOK,...  103 us
    pallas_call x1, Pallas kernels, fit_call(): pl.pallas_call(fit_kernel, out_shape=jax.ShapeDtypeStruct((FEAT, COLS), F...  9.53 us

profile of v6, /device:TPU:1, one launch (start us, length us, event | category | flops | bytes accessed | tf_op | source)
XLA Modules:
  0.0 112.4 jit_solution(2556177656426083560)
XLA Ops:
  0.0 102.7 %rotate_gather.1 = (bf16[4,4,128,896]{3,2,1,0:T(8,128)(2,1)}, bf16[4,4,640,128]{3,2,1,0:T(8,128)(2,1)}) custom-call(bf16[128,3456]{1,0:T(8,128)(2,1)} %gate_hbm.1, bf16[128,3456]{1,0:T(8,128)(2,1)} %up_hbm.1, bf16[128,640]{1,0:T(8,128)(2,1)} %grad_hbm.1, bf16[3456,896]{1,0:T(8,128)(2,1)} %bin_hbm.1, bf16[640,5120]{1,0:T(8,128)(2,1)} %bout_hbm.1), custom_call_target="tpu_custom_call" | custom-call | tf_op jit(solution)/shard_map/rotate_gather/pallas_call | solution.py:444
  102.7 9.5 %sequence_products.1 = f32[640,896]{1,0:T(8,128)} custom-call(s32[8]{0:T(128)} %lengths.1, bf16[4,4,128,896]{3,2,1,0:T(8,128)(2,1)} %get-tuple-element.7.r_hbm, bf16[4,4,640,128]{3,2,1,0:T(8,128)(2,1)} %get-tuple-element.8.gt_hbm), custom_call_target="tpu_custom_call" | custom-call | tf_op jit(solution)/shard_map/sequence_products/pallas_call | solution.py:546
